TPU v7x, 32 devices: a whole 2x2x4 slice. The times are simulated.
32 devices in a mesh: site: 8 (over y, x, core), tm: 4 (over z).
Axes of the slice: x: 2, y: 2, z: 4, core: 2. Of those that a mesh axis runs over, the one named last changes fastest.
Arguments:
- site_field: bfloat16 [32768, 1024], P('site', 'tm'), may hold values from -3 to 3
- positions: bfloat16 [2, 32768], P(None, 'site'), may hold values from 0 to 4
- site_scale: bfloat16 [32768], P('site'), may hold values from 0.5 to 2
- neighbor_blocks: int32 [256, 16], P('site'), may hold values from 0 to 255, as said below
- neighbor_count: int32 [256], P('site'), may hold values from 1 to 16, as said below
- lag_values: float32 [65], replicated, may hold values from 0.05 to 0.25
- time_band: int32 [1024], replicated, may hold values from 1 to 64, as said below
Outputs:
- product: bfloat16 [32768, 1024], P('site', 'tm')
Inputs may be any that keep to these rules, and one draw needn't show every extreme that they name: `neighbor_blocks`: block b lies on device b // 32 of the site axis. A block that lists a block of another device names one of the 2 blocks of that device nearest to its own: those with the lowest indices within it when that device comes later along the axis, the highest when it comes earlier. On every device the first block's first 2 slots name all 2 such blocks of the next device (of the first device, for the last). Slots from neighbor_count onward are unused. The first block of every device uses all 16. `time_band`: some time step has 64.
All inputs are finite; a program needn't handle non-finite values.
Results may differ from a plain program's by a relative error of at most 0.0062.
Values may be sent and summed in bfloat16 or wider, within the bound.
A program may use at most 64 MiB of HBM per device.

v0:
```python
import jax
import jax.numpy as jnp
from jax import lax
from jax.sharding import PartitionSpec as P

BS = 128
KNB = 16
CAP = 2
BMAX = 64


turn_blocks = 4


def with_halo(array, sides, width):
    for axis, dim in sides:
        size, length = (lax.axis_size(axis), array.shape[dim])
        up = [(i, (i + 1) % size) for i in range(size - 1)]
        down = [(j, i) for i, j in up]
        last = lax.slice_in_dim(array, length - width, length, axis=dim)
        leading = lax.slice_in_dim(array, 0, width, axis=dim)
        before = lax.ppermute(last, axis, up)
        after = lax.ppermute(leading, axis, down)
        array = jnp.concatenate([before, array, after], axis=dim)
    return array


def kernel_tiles(row_geo, col_geo):
    row_geo = row_geo.astype(jnp.float32)
    col_geo = col_geo.astype(jnp.float32)
    across = row_geo[..., 0, :, None] - col_geo[..., 0, None, :]
    upward = row_geo[..., 1, :, None] - col_geo[..., 1, None, :]
    distance = jnp.sqrt(across * across + upward * upward)
    scaled = distance / 3.0
    tapering = jnp.maximum(1.0 - scaled, 0.0) ** 4 * (1.0 + 4.0 * scaled)
    return row_geo[..., 2, :, None] * col_geo[..., 2, None, :] * jnp.exp(distance * -5.0) * tapering


def lag_table(lag_values, row_band, col_band, offset):
    row_total = row_band.shape[-1]
    column_total = col_band.shape[-1]
    span_total = row_total + column_total - 1
    shifts = jnp.arange(span_total, dtype=jnp.int32) - (column_total - 1) - offset
    lag_series = jnp.abs(shifts)
    levels = jnp.arange(lag_values.shape[0], dtype=jnp.int32)
    series = jnp.sum(
        jnp.where(lag_series[:, None] == levels[None, :], lag_values[None, :], 0.0), axis=1
    )
    repeated = jnp.tile(series, row_total + 1)[: row_total * (span_total + 1)].reshape(
        row_total, span_total + 1
    )
    values = repeated[:, :column_total][:, ::-1]
    lag_grid = jnp.abs(
        jnp.arange(row_total, dtype=jnp.int32)[:, None]
        - offset
        - jnp.arange(column_total, dtype=jnp.int32)[None, :]
    )
    band_limit = jnp.minimum(row_band[..., :, None], col_band[..., None, :])
    return jnp.where(lag_grid <= band_limit, values, 0.0).astype(jnp.bfloat16)


def group_terms(pool_values, pool_geometry, own_geometry, slot_index, slot_live):
    kernel_block = kernel_tiles(own_geometry[:, None], pool_geometry[slot_index])
    kernel_block = jnp.where(slot_live[:, :, None, None], kernel_block, 0.0).astype(jnp.bfloat16)
    return jnp.einsum(
        "gkij,gkjt->git", kernel_block, pool_values[slot_index], preferred_element_type=jnp.float32
    )


def shards(
    site_field, positions, site_scale, neighbor_blocks, neighbor_count, lag_values, time_band
):
    site_count = lax.axis_size("site")
    my_site = lax.axis_index("site")
    block_count = neighbor_count.shape[0]
    time_width = site_field.shape[1]
    blocks = site_field.reshape(block_count, BS, time_width)
    geometry = (
        jnp.stack([positions[0], positions[1], site_scale])
        .reshape(3, block_count, BS)
        .transpose(1, 0, 2)
    )
    owner_site = neighbor_blocks // block_count
    within = neighbor_blocks % block_count
    window_slot = jnp.where(owner_site > my_site, within, within - (block_count - CAP))
    head_values = blocks[:CAP]
    tail_values = blocks[block_count - CAP :]
    head_geometry = geometry[:CAP]
    tail_geometry = geometry[block_count - CAP :]
    lower = (jnp.arange(site_count, dtype=jnp.int32) < my_site)[:, None, None, None]
    send_values = jnp.where(lower, head_values[None], tail_values[None]).reshape(
        site_count * CAP, BS, time_width
    )
    send_geometry = jnp.where(lower, head_geometry[None], tail_geometry[None]).reshape(
        site_count * CAP, 3, BS
    )
    got_values, got_geometry = (
        lax.all_to_all(send_values, "site", split_axis=0, concat_axis=0, tiled=True),
        lax.all_to_all(send_geometry, "site", split_axis=0, concat_axis=0, tiled=True),
    )
    remote_index = block_count + owner_site * CAP + window_slot
    slot_index = jnp.where(owner_site == my_site, within, remote_index)
    pool_values = jnp.concatenate([blocks, got_values])
    pool_geometry = jnp.concatenate([geometry, got_geometry])
    slot_live = jnp.arange(KNB, dtype=jnp.int32)[None, :] < neighbor_count[:, None]
    turn_total = block_count // turn_blocks

    def one_turn(members):
        own_geometry, turn_index, turn_live = members
        return group_terms(pool_values, pool_geometry, own_geometry, turn_index, turn_live).astype(
            jnp.bfloat16
        )

    space_field = lax.map(
        one_turn,
        (
            geometry.reshape(turn_total, turn_blocks, 3, BS),
            slot_index.reshape(turn_total, turn_blocks, KNB),
            slot_live.reshape(turn_total, turn_blocks, KNB),
        ),
    ).reshape(block_count * BS, time_width)
    padded = with_halo(space_field, (("tm", 1),), BMAX)
    start = lax.axis_index("tm") * time_width
    row_band = lax.dynamic_slice_in_dim(
        jnp.pad(time_band, (BMAX, BMAX)), start, time_width + 2 * BMAX
    )
    col_band = lax.dynamic_slice_in_dim(time_band, start, time_width)
    band_table = lag_table(lag_values, row_band, col_band, BMAX)
    product = jnp.dot(padded, band_table, preferred_element_type=jnp.float32).astype(jnp.bfloat16)
    return product


def solution(mesh):
    placed = (P("site", "tm"), P(None, "site"), P("site"), P("site", None), P("site"), P(), P())
    return jax.shard_map(
        shards, mesh=mesh, in_specs=placed, out_specs=P("site", "tm"), check_vma=False
    )
```

profile of v0, /device:TPU:2, one launch (start us, length us, event | category | flops | bytes accessed | tf_op | source)
XLA Modules:
  0.0 142.3 jit_solution(3079209101685632333)
XLA Ops:
  2.3 4.3 %all-to-all-start = ((bf16[16,3,128]{2,1,0:T(4,128)(2,1)}), bf16[16,3,128]{2,1,0:T(4,128)(2,1)S(1)}, u32[]{:S(2)}, u32[]{:S(2)}) async-start(bf16[16,3,128]{2,1,0:T(4,128)(2,1)} %bitcast_select_fusion.1), calls=%async_computation | async-start | bytes 32768 | tf_op jit(solution)/shard_map/all_to_all | solution.py:99
  6.6 1.0 fusion.39
  7.6 1.1 bitcast_select_fusion
  8.7 1.2 all-to-all-done
  9.9 4.9 %all-to-all-start.1 = ((bf16[16,128,256]{2,1,0:T(8,128)(2,1)}), bf16[16,128,256]{2,1,0:T(8,128)(2,1)S(1)}, u32[]{:S(2)}, u32[]{:S(2)}) async-start(bf16[16,128,256]{2,1,0:T(8,128)(2,1)} %bitcast_select_fusion), calls=%async_computation.1 | async-start | bytes 2097152 | tf_op jit(solution)/shard_map/all_to_all | solution.py:98
  16.5 12.3 %all-to-all-done.1 = bf16[16,128,256]{2,1,0:T(8,128)(2,1)S(1)} async-done(((bf16[16,128,256]{2,1,0:T(8,128)(2,1)}), bf16[16,128,256]{2,1,0:T(8,128)(2,1)S(1)}, u32[]{:S(2)}, u32[]{:S(2)}) %all-to-all-start.1) | async-done | bytes 1048608 | tf_op jit(solution)/shard_map/all_to_all | solution.py:98
  28.7 1.0 copy-done
  29.7 2.2 %pad_maximum_fusion = bf16[48,128,256]{2,1,0:T(8,128)(2,1)S(1)} fusion(bf16[16,128,256]{2,1,0:T(8,128)(2,1)} %copy-done, bf16[32,128,256]{2,1,0:T(8,128)(2,1)} %bitcast.85), kind=kLoop, calls=%fused_computation.33 | loop fusion | flops 1572864 | bytes 6291456 | tf_op jit(solution)/shard_map/concatenate | solution.py:103
  31.9 82.4 %while.12 = (s32[]{:T(128)}, bf16[8,4,128,256]{3,2,1,0:T(8,128)(2,1)}, pred[8,4,16]{2,1,0:T(4,128)(4,1)S(1)}, bf16[8,4,3,128]{3,1,0,2:T(4,128)(2,1)S(1)}, s32[8,...) while((s32[]{:T(128)}, ...), condition=%wide.region_1.2_spmd, body=%wide.region_0.1_spmd.sunk | while | flops 556927680 | bytes 13272609 | solution.py:114
  32.8 2.8 %gather_fusion = bf16[64,128,256]{2,1,0:T(8,128)(2,1)} fusion(bf16[48,128,256]{2,1,0:T(8,128)(2,1)S(1)} %get-tuple-element.223, s32[1024]{0:T(1024)S(1)} %pad_clamp_fusion.2), kind=kCustom, calls=%fused_computation.1.clone.1 | custom fusion | bytes 8388864 | tf_op jit(solution)/shard_map/while/body/eval_jaxpr/gather | solution.py:66
  35.5 6.7 %fusion.47 = bf16[8,4,128,256]{3,2,1,0:T(8,128)(2,1)} fusion(bf16[8,4,128,256]{3,2,1,0:T(8,128)(2,1)} %get-tuple-element.210, s32[]{:T(128)} %get-tuple-element.209, bf16[4,16,128,256]{3,2,1,0:T(8,128)(2,1)} %bitcast.83, f32[4,16,128]{2,1,0:T(8,128)S(1)} %bitcast.89, f32[4,128]{1,0:T(4,128)S(1)} %get-tuple-element.196, ...), kind=kOutput, calls=%fused_computation.19.clone.1 | convolution fusion | flops 556924928 | bytes 4561472 | tf_op jit(solution)/shard_map/while/body/eval_jaxpr/gkij,gkjt->git/dot_general | solution.py:65
  43.1 2.8 %gather_fusion = bf16[64,128,256]{2,1,0:T(8,128)(2,1)} fusion(bf16[48,128,256]{2,1,0:T(8,128)(2,1)S(1)} %get-tuple-element.223, s32[1024]{0:T(1024)S(1)} %pad_clamp_fusion.2), kind=kCustom, calls=%fused_computation.1.clone.1 | custom fusion | bytes 8388864 | tf_op jit(solution)/shard_map/while/body/eval_jaxpr/gather | solution.py:66
  45.8 6.7 %fusion.47 = bf16[8,4,128,256]{3,2,1,0:T(8,128)(2,1)} fusion(bf16[8,4,128,256]{3,2,1,0:T(8,128)(2,1)} %get-tuple-element.210, s32[]{:T(128)} %get-tuple-element.209, bf16[4,16,128,256]{3,2,1,0:T(8,128)(2,1)} %bitcast.83, f32[4,16,128]{2,1,0:T(8,128)S(1)} %bitcast.89, f32[4,128]{1,0:T(4,128)S(1)} %get-tuple-element.196, ...), kind=kOutput, calls=%fused_computation.19.clone.1 | convolution fusion | flops 556924928 | bytes 4561472 | tf_op jit(solution)/shard_map/while/body/eval_jaxpr/gkij,gkjt->git/dot_general | solution.py:65
  53.4 2.8 %gather_fusion = bf16[64,128,256]{2,1,0:T(8,128)(2,1)} fusion(bf16[48,128,256]{2,1,0:T(8,128)(2,1)S(1)} %get-tuple-element.223, s32[1024]{0:T(1024)S(1)} %pad_clamp_fusion.2), kind=kCustom, calls=%fused_computation.1.clone.1 | custom fusion | bytes 8388864 | tf_op jit(solution)/shard_map/while/body/eval_jaxpr/gather | solution.py:66
  56.1 6.7 %fusion.47 = bf16[8,4,128,256]{3,2,1,0:T(8,128)(2,1)} fusion(bf16[8,4,128,256]{3,2,1,0:T(8,128)(2,1)} %get-tuple-element.210, s32[]{:T(128)} %get-tuple-element.209, bf16[4,16,128,256]{3,2,1,0:T(8,128)(2,1)} %bitcast.83, f32[4,16,128]{2,1,0:T(8,128)S(1)} %bitcast.89, f32[4,128]{1,0:T(4,128)S(1)} %get-tuple-element.196, ...), kind=kOutput, calls=%fused_computation.19.clone.1 | convolution fusion | flops 556924928 | bytes 4561472 | tf_op jit(solution)/shard_map/while/body/eval_jaxpr/gkij,gkjt->git/dot_general | solution.py:65
  63.6 2.8 %gather_fusion = bf16[64,128,256]{2,1,0:T(8,128)(2,1)} fusion(bf16[48,128,256]{2,1,0:T(8,128)(2,1)S(1)} %get-tuple-element.223, s32[1024]{0:T(1024)S(1)} %pad_clamp_fusion.2), kind=kCustom, calls=%fused_computation.1.clone.1 | custom fusion | bytes 8388864 | tf_op jit(solution)/shard_map/while/body/eval_jaxpr/gather | solution.py:66
  66.4 6.7 %fusion.47 = bf16[8,4,128,256]{3,2,1,0:T(8,128)(2,1)} fusion(bf16[8,4,128,256]{3,2,1,0:T(8,128)(2,1)} %get-tuple-element.210, s32[]{:T(128)} %get-tuple-element.209, bf16[4,16,128,256]{3,2,1,0:T(8,128)(2,1)} %bitcast.83, f32[4,16,128]{2,1,0:T(8,128)S(1)} %bitcast.89, f32[4,128]{1,0:T(4,128)S(1)} %get-tuple-element.196, ...), kind=kOutput, calls=%fused_computation.19.clone.1 | convolution fusion | flops 556924928 | bytes 4561472 | tf_op jit(solution)/shard_map/while/body/eval_jaxpr/gkij,gkjt->git/dot_general | solution.py:65
  73.9 2.8 %gather_fusion = bf16[64,128,256]{2,1,0:T(8,128)(2,1)} fusion(bf16[48,128,256]{2,1,0:T(8,128)(2,1)S(1)} %get-tuple-element.223, s32[1024]{0:T(1024)S(1)} %pad_clamp_fusion.2), kind=kCustom, calls=%fused_computation.1.clone.1 | custom fusion | bytes 8388864 | tf_op jit(solution)/shard_map/while/body/eval_jaxpr/gather | solution.py:66
  76.7 6.7 %fusion.47 = bf16[8,4,128,256]{3,2,1,0:T(8,128)(2,1)} fusion(bf16[8,4,128,256]{3,2,1,0:T(8,128)(2,1)} %get-tuple-element.210, s32[]{:T(128)} %get-tuple-element.209, bf16[4,16,128,256]{3,2,1,0:T(8,128)(2,1)} %bitcast.83, f32[4,16,128]{2,1,0:T(8,128)S(1)} %bitcast.89, f32[4,128]{1,0:T(4,128)S(1)} %get-tuple-element.196, ...), kind=kOutput, calls=%fused_computation.19.clone.1 | convolution fusion | flops 556924928 | bytes 4561472 | tf_op jit(solution)/shard_map/while/body/eval_jaxpr/gkij,gkjt->git/dot_general | solution.py:65
  84.2 2.8 %gather_fusion = bf16[64,128,256]{2,1,0:T(8,128)(2,1)} fusion(bf16[48,128,256]{2,1,0:T(8,128)(2,1)S(1)} %get-tuple-element.223, s32[1024]{0:T(1024)S(1)} %pad_clamp_fusion.2), kind=kCustom, calls=%fused_computation.1.clone.1 | custom fusion | bytes 8388864 | tf_op jit(solution)/shard_map/while/body/eval_jaxpr/gather | solution.py:66
  87.0 6.7 %fusion.47 = bf16[8,4,128,256]{3,2,1,0:T(8,128)(2,1)} fusion(bf16[8,4,128,256]{3,2,1,0:T(8,128)(2,1)} %get-tuple-element.210, s32[]{:T(128)} %get-tuple-element.209, bf16[4,16,128,256]{3,2,1,0:T(8,128)(2,1)} %bitcast.83, f32[4,16,128]{2,1,0:T(8,128)S(1)} %bitcast.89, f32[4,128]{1,0:T(4,128)S(1)} %get-tuple-element.196, ...), kind=kOutput, calls=%fused_computation.19.clone.1 | convolution fusion | flops 556924928 | bytes 4561472 | tf_op jit(solution)/shard_map/while/body/eval_jaxpr/gkij,gkjt->git/dot_general | solution.py:65
  94.5 2.8 %gather_fusion = bf16[64,128,256]{2,1,0:T(8,128)(2,1)} fusion(bf16[48,128,256]{2,1,0:T(8,128)(2,1)S(1)} %get-tuple-element.223, s32[1024]{0:T(1024)S(1)} %pad_clamp_fusion.2), kind=kCustom, calls=%fused_computation.1.clone.1 | custom fusion | bytes 8388864 | tf_op jit(solution)/shard_map/while/body/eval_jaxpr/gather | solution.py:66
  97.3 6.7 %fusion.47 = bf16[8,4,128,256]{3,2,1,0:T(8,128)(2,1)} fusion(bf16[8,4,128,256]{3,2,1,0:T(8,128)(2,1)} %get-tuple-element.210, s32[]{:T(128)} %get-tuple-element.209, bf16[4,16,128,256]{3,2,1,0:T(8,128)(2,1)} %bitcast.83, f32[4,16,128]{2,1,0:T(8,128)S(1)} %bitcast.89, f32[4,128]{1,0:T(4,128)S(1)} %get-tuple-element.196, ...), kind=kOutput, calls=%fused_computation.19.clone.1 | convolution fusion | flops 556924928 | bytes 4561472 | tf_op jit(solution)/shard_map/while/body/eval_jaxpr/gkij,gkjt->git/dot_general | solution.py:65
  104.8 2.8 %gather_fusion = bf16[64,128,256]{2,1,0:T(8,128)(2,1)} fusion(bf16[48,128,256]{2,1,0:T(8,128)(2,1)S(1)} %get-tuple-element.223, s32[1024]{0:T(1024)S(1)} %pad_clamp_fusion.2), kind=kCustom, calls=%fused_computation.1.clone.1 | custom fusion | bytes 8388864 | tf_op jit(solution)/shard_map/while/body/eval_jaxpr/gather | solution.py:66
  107.6 6.7 %fusion.47 = bf16[8,4,128,256]{3,2,1,0:T(8,128)(2,1)} fusion(bf16[8,4,128,256]{3,2,1,0:T(8,128)(2,1)} %get-tuple-element.210, s32[]{:T(128)} %get-tuple-element.209, bf16[4,16,128,256]{3,2,1,0:T(8,128)(2,1)} %bitcast.83, f32[4,16,128]{2,1,0:T(8,128)S(1)} %bitcast.89, f32[4,128]{1,0:T(4,128)S(1)} %get-tuple-element.196, ...), kind=kOutput, calls=%fused_computation.19.clone.1 | convolution fusion | flops 556924928 | bytes 4561472 | tf_op jit(solution)/shard_map/while/body/eval_jaxpr/gkij,gkjt->git/dot_general | solution.py:65
  114.3 2.9 %copy.27 = bf16[4096,256]{0,1:T(8,128)(2,1)S(1)} copy(bf16[4096,256]{1,0:T(8,128)(2,1)} %bitcast.86) | data formatting | bytes 4194304 | tf_op jit(solution)/shard_map/reshape | solution.py:121
  117.2 1.0 fusion.38
  118.3 4.3 %collective-permute-start = (bf16[4096,64]{0,1:T(8,128)(2,1)}, bf16[4096,64]{0,1:T(8,128)(2,1)}, u32[]{:S(2)}, u32[]{:S(2)}) collective-permute-start(bf16[4096,64]{0,1:T(8,128)(2,1)} %get-tuple-element.136), channel_id=1, source_target_pairs={{0,1},{1,2},{2,3},{4,5},{5,6},{6,7},{8,9},{9,10},{10,11},{12,13},{... | collective-permute-start | bytes 1572872 | tf_op jit(solution)/shard_map/ppermute | solution.py:22
  122.6 1.3 collective-permute-start.1
  126.3 7.2 %collective-permute-done = bf16[4096,64]{0,1:T(8,128)(2,1)} collective-permute-done((bf16[4096,64]{0,1:T(8,128)(2,1)}, bf16[4096,64]{0,1:T(8,128)(2,1)}, u32[]{:S(2)}, u32[]{:S(2)}) %collective-permute-start) | collective-permute-done | bytes 524320 | tf_op jit(solution)/shard_map/ppermute | solution.py:22
  133.4 4.9 %collective-permute-done.1 = bf16[4096,64]{0,1:T(8,128)(2,1)} collective-permute-done((bf16[4096,64]{0,1:T(8,128)(2,1)}, bf16[4096,64]{0,1:T(8,128)(2,1)}, u32[]{:S(2)}, u32[]{:S(2)}) %collective-permute-start.1) | collective-permute-done | bytes 524320 | tf_op jit(solution)/shard_map/ppermute | solution.py:23
  138.4 3.9 %convolution_convert_fusion = bf16[4096,256]{1,0:T(8,128)(2,1)} fusion(bf16[4096,64]{0,1:T(8,128)(2,1)} %collective-permute-done.1, bf16[4096,256]{0,1:T(8,128)(2,1)S(1)} %copy.27, bf16[4096,64]{0,1:T(8,128)(2,1)} %collective-permute-done, bf16[384,256]{1,0:T(8,128)(2,1)S(1)} %rev.3, s32[256]{0:T(256)S(1)} %dynamic_slice.28, ...), kind=kOutput, calls=%fused_computation.32 | convolution fusion | flops 816283648 | bytes 5443584 | tf_op jit(solution)/shard_map/dot_general | solution.py:129
  (96 shorter events, 13.0 us)
Async XLA Ops:
  2.3 7.5 %all-to-all-start = ((bf16[16,3,128]{2,1,0:T(4,128)(2,1)}), bf16[16,3,128]{2,1,0:T(4,128)(2,1)S(1)}, u32[]{:S(2)}, u32[]{:S(2)}) async-start(bf16[16,3,128]{2,1,0:T(4,128)(2,1)} %bitcast_select_fusion.1), calls=%async_computation | async-start | bytes 32768 | tf_op jit(solution)/shard_map/all_to_all | solution.py:99
  9.9 18.8 %all-to-all-start.1 = ((bf16[16,128,256]{2,1,0:T(8,128)(2,1)}), bf16[16,128,256]{2,1,0:T(8,128)(2,1)S(1)}, u32[]{:S(2)}, u32[]{:S(2)}) async-start(bf16[16,128,256]{2,1,0:T(8,128)(2,1)} %bitcast_select_fusion), calls=%async_computation.1 | async-start | bytes 2097152 | tf_op jit(solution)/shard_map/all_to_all | solution.py:98
  28.7 1.0 copy-start
  114.3 9.6 %copy-start.2 = (f32[65]{0:T(128)S(1)}, f32[65]{0:T(128)}, u32[]{:S(2)}) copy-start(f32[65]{0:T(128)} %param.14) | copy-start | bytes 784
  117.2 8.9 %copy-start.1 = (s32[1024]{0:T(1024)S(1)}, s32[1024]{0:T(1024)}, u32[]{:S(2)}) copy-start(s32[1024]{0:T(1024)} %param.15) | copy-start | bytes 12292
  118.3 15.2 %collective-permute-start = (bf16[4096,64]{0,1:T(8,128)(2,1)}, bf16[4096,64]{0,1:T(8,128)(2,1)}, u32[]{:S(2)}, u32[]{:S(2)}) collective-permute-start(bf16[4096,64]{0,1:T(8,128)(2,1)} %get-tuple-element.136), channel_id=1, source_target_pairs={{0,1},{1,2},{2,3},{4,5},{5,6},{6,7},{8,9},{9,10},{10,11},{12,13},{... | collective-permute-start | bytes 1572872 | tf_op jit(solution)/shard_map/ppermute | solution.py:22
  122.6 15.8 %collective-permute-start.1 = (bf16[4096,64]{0,1:T(8,128)(2,1)}, bf16[4096,64]{0,1:T(8,128)(2,1)}, u32[]{:S(2)}, u32[]{:S(2)}) collective-permute-start(bf16[4096,64]{0,1:T(8,128)(2,1)} %get-tuple-element.137), channel_id=1, source_target_pairs={{1,0},{2,1},{3,2},{5,4},{6,5},{7,6},{9,8},{10,9},{11,10},{13,12},{... | collective-permute-start | bytes 1572872 | tf_op jit(solution)/shard_map/ppermute | solution.py:23
where the time goes:
time: 143 us; the launch traced here: 142 us
  matrix products  57.4 us (40%)
  local copies, waits for them, and re-layouts  38.5 us (27%)
  waiting for transfers between devices  25.6 us (18%)
  starting transfers between devices  14.8 us (10%)
  other arithmetic  5.84 us (4%)
    dot_general x8, matrix products, group_terms(): jnp.einsum('gkij,gkjt->git', kernel_block, pool_values[slot_index], prefe...  53.5 us
    gather x8, local copies, waits for them, and re-layouts, group_terms(): pool_values[slot_index]  22.1 us
    all_to_all x1, waiting for transfers between devices, shards(): lax.all_to_all(send_values, 'site', split_axis=0, concat_axis=0, tiled=True)  12.3 us
    ppermute x1, waiting for transfers between devices, with_halo(): before = lax.ppermute(last, axis, up)  7.18 us
    gather x8, local copies, waits for them, and re-layouts, group_terms(): pool_geometry[slot_index]  5.26 us
    ppermute x1, waiting for transfers between devices, with_halo(): after = lax.ppermute(leading, axis, down)  4.94 us
    all_to_all x1, starting transfers between devices, shards(): lax.all_to_all(send_values, 'site', split_axis=0, concat_axis=0, tiled=True)  4.93 us
    ppermute x1, starting transfers between devices, with_halo(): before = lax.ppermute(last, axis, up)  4.31 us
  transfers between devices with their start and end apart: 4, of which 4 were waited for; matrix products, arithmetic and copies ran while one was open for 4% of the time, Pallas kernels for 0%

commit v1 on v0

v1 whole, which is shorter than its diff:
```python
import functools
import math

import jax
import jax.numpy as jnp
from jax import lax
from jax.experimental import pallas as pl
from jax.experimental.pallas import tpu as pltpu
from jax.sharding import PartitionSpec as P

CAP = 2
MESH = pl.DeviceIdType.MESH
f32 = jnp.float32
bf16 = jnp.bfloat16


def table_kernel(series_ref, band_ref, mid_ref, halo_ref):
    width = mid_ref.shape[0]
    reach = halo_ref.shape[1] // 2
    total = width + 2 * reach
    base = jnp.broadcast_to(series_ref[...], (total, series_ref.shape[1]))
    values = pltpu.roll(base, 0, 1, stride=1, stride_axis=0)[:, :width]
    turned = jnp.transpose(band_ref[...])
    columns = jnp.concatenate(
        [jnp.broadcast_to(turned[:, j : j + 1], (128, width)) for j in range(total // 128)]
    )
    row = jnp.concatenate([band_ref[pl.ds(total // 128 + j, 1), :] for j in range(width // 128)], 1)
    lag = jnp.abs(
        lax.broadcasted_iota(jnp.int32, (total, width), 0)
        - reach
        - lax.broadcasted_iota(jnp.int32, (total, width), 1)
    ).astype(f32)
    table = jnp.where(lag <= jnp.minimum(columns, row), values, 0.0).astype(bf16)
    first, last = table[:reach], table[reach + width :]
    mid_ref[...] = table[reach : reach + width]
    halo_ref[0] = jnp.concatenate([first, last])
    halo_ref[1] = jnp.concatenate([last, first])


def exchange_kernel(
    site_total, time_total, field, mid, halo, places, scale, pool, geo,
    to_right, to_left, from_left, from_right, scales, edges,
    zsend, zrecv, gsend, grecv, psend, precv,
):
    site, step = lax.axis_index("site"), lax.axis_index("tm")
    rows, width = field.shape
    blocks = scale.shape[0]
    size = rows // blocks
    group = CAP * size
    chunks = rows // (2 * group)
    reach = width // 4
    owned = 2 * blocks

    barrier = pltpu.get_barrier_semaphore()
    for o in range(1, site_total):
        pl.semaphore_signal(
            barrier, inc=1, device_id={"site": lax.rem(site + o, site_total)}, device_id_type=MESH
        )

    for shift in (1, time_total - 1):
        pl.semaphore_signal(
            barrier, inc=1, device_id={"tm": lax.rem(step + shift, time_total)}, device_id_type=MESH
        )

    lane = lax.broadcasted_iota(jnp.int32, (group, 128), 1) < reach

    def pack(c):
        here = pl.ds(pl.multiple_of(c * group, group), group)
        there = pl.ds(pl.multiple_of(rows - (c + 1) * group, group), group)
        right_a = field[here, pl.ds(width - 128, 128)].astype(f32)
        right_b = field[there, pl.ds(width - 128, 128)].astype(f32)
        left_a = field[here, pl.ds(0, 128)].astype(f32)
        left_b = field[there, pl.ds(0, 128)].astype(f32)
        to_right[here, :] = jnp.where(lane, pltpu.roll(right_a, 64, 1), right_b).astype(bf16)
        to_left[here, :] = jnp.where(lane, left_b, pltpu.roll(left_a, 64, 1)).astype(bf16)

    pack(0)
    for k in range(2):
        start = k * (blocks - CAP)
        for j in range(2):
            edges[k, pl.ds(j * CAP, CAP), :] = places[pl.ds(j * blocks + start, CAP), :]
        edges[k, pl.ds(2 * CAP, 8 - 2 * CAP), :] = jnp.zeros((8 - 2 * CAP, 128), f32)

    pl.semaphore_wait(barrier, site_total + 1)

    pieces = [(0, 1), (1, chunks // 2), (chunks // 2, chunks)]

    def sideways(n, right):
        first, last = pieces[n]
        span = pl.ds(first * group, (last - first) * group)
        way = 0 if right else 1
        return pltpu.make_async_remote_copy(
            src_ref=(to_right if right else to_left).at[span],
            dst_ref=(from_left if right else from_right).at[span],
            send_sem=zsend.at[way, n],
            recv_sem=zrecv.at[way, n],
            device_id={"tm": (step + 1) if right else (step - 1)},
            device_id_type=MESH,
        )

    def send(n):
        @pl.when(step < time_total - 1)
        def _():
            sideways(n, True).start()

        @pl.when(step > 0)
        def _():
            sideways(n, False).start()

    def receive(n):
        @pl.when(step > 0)
        def _():
            sideways(n, True).wait_recv()

        @pl.when(step < time_total - 1)
        def _():
            sideways(n, False).wait_recv()

    send(0)

    def points(o):
        later = 1 - (site + o) // site_total
        return pltpu.make_async_remote_copy(
            src_ref=edges.at[later],
            dst_ref=geo.at[pl.ds(owned + 8 * site, 8)],
            send_sem=psend.at[o - 1],
            recv_sem=precv.at[o - 1],
            device_id={"site": lax.rem(site + o, site_total)},
            device_id_type=MESH,
        )

    for o in range(1, site_total):
        points(o).start()

    for n in range(1, len(pieces)):
        lax.fori_loop(pieces[n][0], pieces[n][1], lambda c, _: (pack(c), 0)[1], 0)
        send(n)

    geo[pl.ds(0, owned), :] = places[...]

    @pl.when(step == 0)
    def _():
        from_left[...] = jnp.zeros_like(from_left)

    @pl.when(step == time_total - 1)
    def _():
        from_right[...] = jnp.zeros_like(from_right)

    turned = jnp.transpose(scale[...])
    for b in range(blocks):
        scales[pl.ds(b * size, size), :] = jnp.broadcast_to(turned[:, b : b + 1], (size, 128))

    def smooth(c):
        here = pl.ds(pl.multiple_of(c * group, group), group)
        there = pl.ds(pl.multiple_of(rows - (c + 1) * group, group), group)
        left = from_left[here, :]
        right = from_right[here, :]
        for span, first, second, k in ((here, left, right, 0), (there, right, left, 1)):
            beside = jnp.where(lane, first.astype(f32), second.astype(f32)).astype(bf16)
            total = jnp.dot(field[span, :], mid[...], preferred_element_type=f32)
            total = total + jnp.dot(beside, halo[k], preferred_element_type=f32)
            weight = scales[span, :]
            pool[span, :] = (total * jnp.concatenate([weight] * (width // 128), 1)).astype(bf16)

    def across(o):
        later = 1 - (site + o) // site_total
        return pltpu.make_async_remote_copy(
            src_ref=pool.at[pl.ds(pl.multiple_of(later * (rows - group), group), group)],
            dst_ref=pool.at[pl.ds(pl.multiple_of(rows + site * group, group), group)],
            send_sem=gsend.at[o - 1],
            recv_sem=grecv.at[o - 1],
            device_id={"site": lax.rem(site + o, site_total)},
            device_id_type=MESH,
        )

    receive(0)
    smooth(0)
    for o in range(1, site_total):
        across(o).start()
    for n in range(1, len(pieces)):
        receive(n)
        lax.fori_loop(pieces[n][0], pieces[n][1], lambda c, _: (smooth(c), 0)[1], 0)

    for n in range(len(pieces)):

        @pl.when(step < time_total - 1)
        def _():
            sideways(n, True).wait_send()

        @pl.when(step > 0)
        def _():
            sideways(n, False).wait_send()

    for o in range(1, site_total):
        for copy, into, base, length, sem in (
            (points(o), geo, owned, 8, precv),
            (across(o), pool, rows, group, grecv),
        ):
            copy.wait_send()
            origin = lax.rem(site + site_total - o, site_total)
            landing = into.at[pl.ds(pl.multiple_of(base + origin * length, 8), length)]
            pltpu.make_async_remote_copy(
                src_ref=landing,
                dst_ref=landing,
                send_sem=sem.at[o - 1],
                recv_sem=sem.at[o - 1],
                device_id={"site": origin},
                device_id_type=MESH,
            ).wait_recv()


def combine_kernel(names, counts, pool, geo, scale, out, acc, tiles, across, upward, scales):
    site = lax.axis_index("site")
    blocks = scale.shape[0]
    size = tiles.shape[0]
    slots = names.shape[0] // blocks
    width = out.shape[1]
    for ref, source in (
        (across, geo[pl.ds(0, blocks), :]),
        (upward, geo[pl.ds(blocks, blocks), :]),
        (scales, scale[...]),
    ):
        turned = jnp.transpose(source)
        for b in range(blocks):
            ref[pl.ds(b * size, size), :] = jnp.broadcast_to(turned[:, b : b + 1], (size, 128))

    def named(b, k):
        name = names[b * slots + k]
        owner = name // blocks
        within = name - owner * blocks
        window = jnp.where(owner > site, within, within - (blocks - CAP))
        near = owner == site
        place = jnp.where(near, within, blocks + owner * CAP + window)
        first = jnp.where(near, within, 2 * blocks + 8 * owner + window)
        second = jnp.where(near, blocks + within, 2 * blocks + 8 * owner + window + CAP)
        return place, first, second

    def pair(b, k):
        count = counts[b]
        other = 2 * k + 1
        live = other < count
        return named(b, 2 * k), named(b, jnp.where(live, other, 2 * k)), live

    def build(b, k):
        one, two, live = pair(b, k)
        for j, (slot, weight) in enumerate(((one, 1.0), (two, jnp.where(live, 1.0, 0.0)))):
            x = geo[pl.ds(slot[1], 1), :]
            y = geo[pl.ds(slot[2], 1), :]
            for r in range(0, size, 32):
                span = pl.ds(pl.multiple_of(b * size + r, 32), 32)
                dx = across[span, :] - x
                dy = upward[span, :] - y
                square = dx * dx + dy * dy
                d = square * lax.rsqrt(jnp.maximum(square, 1e-30))
                t = jnp.maximum(1.0 - d, 0.0)
                t = t * t
                value = jnp.exp2(d * (-15.0 * math.log2(math.e))) * (t * t)
                value = value * (d * (4.0 * weight) + weight)
                tiles[pl.ds(r, 32), pl.ds(j * size, size)] = value.astype(bf16)

    def multiply(b, k):
        one, two, _ = pair(b, k)
        values = jnp.concatenate(
            [pool[pl.ds(pl.multiple_of(s[0] * size, size), size), :] for s in (one, two)]
        )
        product = jnp.dot(tiles[...], values, preferred_element_type=f32)
        total = jnp.where(k > 0, acc[...], 0.0) + product
        acc[...] = total
        return total

    def finish(b, total):
        span = pl.ds(pl.multiple_of(b * size, size), size)
        weight = jnp.concatenate([scales[span, :]] * (width // 128), 1)
        out[span, :] = (total * weight).astype(bf16)

    def pairs(b):
        return (counts[b] + 1) // 2

    build(0, 0)

    def block(b, _):
        def inner(k, _):
            multiply(b, k - 1)
            build(b, k)
            return 0

        last = pairs(b)
        lax.fori_loop(1, last, inner, 0)
        finish(b, multiply(b, last - 1))
        build(jnp.minimum(b + 1, blocks - 1), 0)
        return 0

    lax.fori_loop(0, blocks, block, 0)


def shards(
    site_total, time_total,
    site_field, positions, site_scale, neighbor_blocks, neighbor_count, lag_values, time_band,
):
    rows, width = site_field.shape
    blocks, slots = neighbor_blocks.shape
    size = rows // blocks
    reach = lag_values.shape[0] - 1
    group = CAP * size
    places = (positions.astype(f32) * (1.0 / 3.0)).reshape(2 * blocks, size)
    scale = site_scale.astype(f32).reshape(blocks, size)
    series = jnp.concatenate(
        [
            lag_values[reach:],
            jnp.zeros((2 * width - 2 * reach - 1,), f32),
            lag_values[:0:-1],
            lag_values[:reach],
        ]
    ).reshape(1, 2 * width)
    start = lax.axis_index("tm") * width
    padded = jnp.pad(time_band.astype(f32), (reach, reach))
    around = lax.dynamic_slice_in_dim(padded, start, width + 2 * reach)
    total = width + 2 * reach
    band = jnp.concatenate(
        [around, around[reach : reach + width], jnp.zeros((8 * 128 - total - width,), f32)]
    ).reshape(8, 128)
    vmem = pl.BlockSpec(memory_space=pltpu.VMEM)
    smem = pl.BlockSpec(memory_space=pltpu.SMEM)
    mid, halo = pl.pallas_call(
        table_kernel,
        out_shape=[
            jax.ShapeDtypeStruct((width, width), bf16),
            jax.ShapeDtypeStruct((2, 2 * reach, width), bf16),
        ],
        in_specs=[vmem] * 2,
        out_specs=[vmem] * 2,
        name="table",
    )(series, band)
    pool, geo = pl.pallas_call(
        functools.partial(exchange_kernel, site_total, time_total),
        out_shape=[
            jax.ShapeDtypeStruct((rows + site_total * group, width), bf16),
            jax.ShapeDtypeStruct((2 * blocks + 8 * site_total, size), f32),
        ],
        in_specs=[vmem] * 5,
        out_specs=[vmem] * 2,
        scratch_shapes=[
            pltpu.VMEM((rows // 2, 128), bf16),
            pltpu.VMEM((rows // 2, 128), bf16),
            pltpu.VMEM((rows // 2, 128), bf16),
            pltpu.VMEM((rows // 2, 128), bf16),
            pltpu.VMEM((rows, 128), f32),
            pltpu.VMEM((2, 8, 128), f32),
            pltpu.SemaphoreType.DMA((2, 3)),
            pltpu.SemaphoreType.DMA((2, 3)),
            pltpu.SemaphoreType.DMA((site_total - 1,)),
            pltpu.SemaphoreType.DMA((site_total - 1,)),
            pltpu.SemaphoreType.DMA((site_total - 1,)),
            pltpu.SemaphoreType.DMA((site_total - 1,)),
        ],
        compiler_params=pltpu.CompilerParams(
            collective_id=0, has_side_effects=True, vmem_limit_bytes=24 * 2**20
        ),
        name="exchange",
    )(site_field, mid, halo, places, scale)
    return pl.pallas_call(
        combine_kernel,
        out_shape=jax.ShapeDtypeStruct((rows, width), bf16),
        in_specs=[smem] * 2 + [vmem] * 3,
        out_specs=vmem,
        scratch_shapes=[
            pltpu.VMEM((size, width), f32),
            pltpu.VMEM((size, 2 * size), bf16),
            pltpu.VMEM((rows, 128), f32),
            pltpu.VMEM((rows, 128), f32),
            pltpu.VMEM((rows, 128), f32),
        ],
        compiler_params=pltpu.CompilerParams(vmem_limit_bytes=28 * 2**20),
        name="combine",
    )(neighbor_blocks.reshape(-1), neighbor_count, pool, geo, scale)


def solution(mesh):
    placed = (P("site", "tm"), P(None, "site"), P("site"), P("site", None), P("site"), P(), P())
    return jax.shard_map(
        functools.partial(shards, mesh.shape["site"], mesh.shape["tm"]),
        mesh=mesh,
        in_specs=placed,
        out_specs=P("site", "tm"),
        check_vma=False,
    )
```

time: 143 us -> 61.2 us (0.43)
  the two profiles are of different devices: /device:TPU:2 before, /device:TPU:0 now
where the time goes in v1:
time: 61.2 us; the launch traced here: 62.3 us
  Pallas kernels  51.7 us (84%)
  local copies, waits for them, and re-layouts  6.58 us (11%)
  other arithmetic  4.02 us (7%)
    pallas_call x1, Pallas kernels, shards(): pl.pallas_call(combine_kernel, out_shape=jax.ShapeDtypeStruct((rows, widt...  30.3 us
    pallas_call x1, Pallas kernels, shards(): pl.pallas_call(functools.partial(exchange_kernel, site_total, time_total)...  19.8 us
    unnamed x9, local copies, waits for them, and re-layouts  4.17 us
    pallas_call x1, Pallas kernels, shards(): pl.pallas_call(table_kernel, out_shape=[jax.ShapeDtypeStruct((width, widt...  1.61 us
    concatenate x1, other arithmetic, shards(): jnp.concatenate([lag_values[reach:], jnp.zeros((2 * width - 2 * reach - 1...  1.29 us
    slice x1, local copies, waits for them, and re-layouts, shards(): lag_values[reach:]  1.25 us

profile of v1, /device:TPU:0, one launch (start us, length us, event | category | flops | bytes accessed | tf_op | source)
XLA Modules:
  0.0 62.3 jit_solution(17657501489585522437)
XLA Ops:
  0.0 0.0 copy-start.3
  0.0 1.2 %slice.12 = f32[1]{0:T(128)} slice(f32[65]{0:T(128)} %param.12), slice={[64:65]} | slice | bytes 8 | tf_op jit(solution)/shard_map/slice | solution.py:309
  1.3 0.8 %fusion = (f32[64]{0:T(128)S(1)}, f32[64]{0:T(128)S(1)}) fusion(f32[65]{0:T(128)} %param.12), kind=kLoop, calls=%fused_computation.5 | loop fusion | bytes 1024 | tf_op jit(solution)/shard_map/slice | solution.py:311
  2.1 0.1 rev.3
  2.2 1.3 %pad_maximum_fusion = f32[512]{0:T(512)} fusion(f32[64]{0:T(128)S(1)} %get-tuple-element.14, f32[64]{0:T(128)S(1)} %rev.3, f32[383]{0:T(512)S(1)} %broadcast_in_dim.6, f32[1]{0:T(128)} %slice.12), kind=kLoop, calls=%fused_computation.4 | loop fusion | flops 1536 | bytes 4096 | tf_op jit(solution)/shard_map/concatenate | solution.py:307
  3.4 0.7 %convert_element_type.9 = f32[1024]{0:T(1024)S(1)} convert(s32[1024]{0:T(1024)} %param.13) | non-fusion elementwise | flops 1024 | bytes 8192 | tf_op jit(solution)/shard_map/convert_element_type | solution.py:316
  4.1 0.1 pad_dynamic-slice_fusion
  4.2 0.1 slice.15
  4.3 0.6 maximum_bitcast_fusion.band_ref
  4.9 0.7 %bitcast_convert_fusion.scale = f32[32,128]{1,0:T(8,128)S(1)} fusion(bf16[4096]{0:T(1024)(128)(2,1)} %param.9), kind=kLoop, calls=%fused_computation.1 | loop fusion | flops 4096 | bytes 24576 | tf_op jit(solution)/shard_map/reshape | solution.py:306
  5.6 0.8 %copy.8 = s32[32,16]{1,0:T(8,128)S(1)} copy(s32[32,16]{0,1:T(8,128)} %param.10) | data formatting | bytes 4096 | tf_op args[3]
  6.4 0.1 reshape.17.names
  6.4 0.7 %convert_multiply_fusion = f32[2,4096]{1,0:T(2,128)S(1)} fusion(bf16[2,4096]{1,0:T(2,128)(2,1)} %param.8), kind=kLoop, calls=%fused_computation | loop fusion | flops 16384 | bytes 49152 | tf_op jit(solution)/shard_map/mul | solution.py:305
  7.2 1.6 %table.1 = (bf16[256,256]{1,0:T(8,128)(2,1)}, bf16[2,128,256]{2,1,0:T(8,128)(2,1)}) custom-call(f32[1,512]{1,0:T(1,128)} %bitcast.6, f32[8,128]{1,0:T(8,128)} %maximum_bitcast_fusion.band_ref), custom_call_target="tpu_custom_call" | custom-call | tf_op jit(solution)/shard_map/table/pallas_call | solution.py:324
  8.8 0.0 copy-start
  8.8 1.6 %copy-done = bf16[4096,256]{1,0:T(8,128)(2,1)S(1)} copy-done((bf16[4096,256]{1,0:T(8,128)(2,1)S(1)}, bf16[4096,256]{1,0:T(8,128)(2,1)}, u32[]{:S(2)}) %copy-start) | copy-done | bytes 2097176
  10.4 0.0 copy-start.1
  10.4 0.9 %copy-done.1 = bf16[256,256]{1,0:T(8,128)(2,1)S(1)} copy-done((bf16[256,256]{1,0:T(8,128)(2,1)S(1)}, bf16[256,256]{1,0:T(8,128)(2,1)}, u32[]{:S(2)}) %copy-start.1) | copy-done | bytes 131096
  11.3 0.0 copy-start.2
  11.3 0.9 %copy-done.2 = bf16[2,128,256]{2,1,0:T(8,128)(2,1)S(1)} copy-done((bf16[2,128,256]{2,1,0:T(8,128)(2,1)S(1)}, bf16[2,128,256]{2,1,0:T(8,128)(2,1)}, u32[]{:S(2)}) %copy-start.2) | copy-done | bytes 131096
  12.2 19.8 %exchange.1 = (bf16[6144,256]{1,0:T(8,128)(2,1)S(1)}, f32[128,128]{1,0:T(8,128)S(1)}) custom-call(bf16[4096,256]{1,0:T(8,128)(2,1)S(1)} %copy-done, bf16[256,256]{1,0:T(8,128)(2,1)S(1)} %copy-done.1, bf16[2,128,256]{2,1,0:T(8,128)(2,1)S(1)} %copy-done.2, f32[64,128]{1,0:T(8,128)S(1)} %reshape.20.places, f32[32,128]{1,0:T(8,128)S(1)} %bitcast_convert_fusion.scale), custom_call_target="tpu_custom_call" | custom-call | tf_op jit(solution)/shard_map/exchange/pallas_call | solution.py:334
  32.0 0.0 copy-done.3
  32.0 30.3 %combine.1 = bf16[4096,256]{1,0:T(8,128)(2,1)} custom-call(s32[512]{0:T(512)S(1)} %reshape.17.names, s32[32]{0:T(128)S(1)} %copy-done.3, bf16[6144,256]{1,0:T(8,128)(2,1)S(1)} %get-tuple-element.11.pool, f32[128,128]{1,0:T(8,128)S(1)} %get-tuple-element.12.geo, f32[32,128]{1,0:T(8,128)S(1)} %bitcast_convert_fusion.scale), custom_call_target="tpu_custom_call" | custom-call | tf_op jit(solution)/shard_map/combine/pallas_call | solution.py:361
  (3 shorter events, 0.0 us)
Async XLA Ops:
  0.0 32.0 %copy-start.3 = (s32[32]{0:T(128)S(1)}, s32[32]{0:T(128)}, u32[]{:S(2)}) copy-start(s32[32]{0:T(128)} %counts.1) | copy-start | bytes 388
  8.8 1.6 %copy-start = (bf16[4096,256]{1,0:T(8,128)(2,1)S(1)}, bf16[4096,256]{1,0:T(8,128)(2,1)}, u32[]{:S(2)}) copy-start(bf16[4096,256]{1,0:T(8,128)(2,1)} %field.1) | copy-start | bytes 6291460
  10.4 0.9 %copy-start.1 = (bf16[256,256]{1,0:T(8,128)(2,1)S(1)}, bf16[256,256]{1,0:T(8,128)(2,1)}, u32[]{:S(2)}) copy-start(bf16[256,256]{1,0:T(8,128)(2,1)} %get-tuple-element.9.mid) | copy-start | bytes 393220
  11.3 0.9 %copy-start.2 = (bf16[2,128,256]{2,1,0:T(8,128)(2,1)S(1)}, bf16[2,128,256]{2,1,0:T(8,128)(2,1)}, u32[]{:S(2)}) copy-start(bf16[2,128,256]{2,1,0:T(8,128)(2,1)} %get-tuple-element.10.halo) | copy-start | bytes 393220

commit v2 on v1

--- a/solution.py
+++ b/solution.py
@@ -14,31 +14,50 @@
 bf16 = jnp.bfloat16
 
 
-def table_kernel(series_ref, band_ref, mid_ref, halo_ref):
+def table_kernel(lag_ref, band_ref, mid_ref, halo_ref, lags):
+    step = lax.axis_index("tm")
     width = mid_ref.shape[0]
     reach = halo_ref.shape[1] // 2
-    total = width + 2 * reach
-    base = jnp.broadcast_to(series_ref[...], (total, series_ref.shape[1]))
-    values = pltpu.roll(base, 0, 1, stride=1, stride_axis=0)[:, :width]
-    turned = jnp.transpose(band_ref[...])
+    own = width // 128
+    total = width + 256
+    lags[...] = jnp.zeros_like(lags)
+    lags[pl.ds(0, 1), pl.ds(0, reach + 1)] = lag_ref[...]
+    lag_column = jnp.transpose(lags[...])[:, :1]
+    lanes = 2 * width
+    apart = jnp.abs(lax.broadcasted_iota(jnp.int32, (128, lanes), 1) - (lanes - 128))
+    chosen = apart == lax.broadcasted_iota(jnp.int32, (128, lanes), 0)
+    series = jnp.sum(
+        jnp.where(chosen, jnp.broadcast_to(lag_column, (128, lanes)), 0.0), axis=0, keepdims=True
+    )
+    values = pltpu.roll(
+        jnp.broadcast_to(series, (total, lanes)), 0, 1, stride=1, stride_axis=0
+    )[:, :width]
+    most = band_ref.shape[0] - 1
+    before = band_ref[pl.ds(jnp.maximum(step * own - 1, 0), 1), :].astype(f32)
+    after = band_ref[pl.ds(jnp.minimum(step * own + own, most), 1), :].astype(f32)
+    here = [band_ref[pl.ds(step * own + j, 1), :].astype(f32) for j in range(own)]
+    before = jnp.where(step > 0, before, 0.0)
+    after = jnp.where(step * own + own <= most, after, 0.0)
+    gathered = jnp.concatenate([before] + here + [after] + [before] * (8 - own - 2))
+    turned = jnp.transpose(gathered)
     columns = jnp.concatenate(
-        [jnp.broadcast_to(turned[:, j : j + 1], (128, width)) for j in range(total // 128)]
+        [jnp.broadcast_to(turned[:, j : j + 1], (128, width)) for j in range(own + 2)]
     )
-    row = jnp.concatenate([band_ref[pl.ds(total // 128 + j, 1), :] for j in range(width // 128)], 1)
+    row = jnp.concatenate(here, 1)
     lag = jnp.abs(
         lax.broadcasted_iota(jnp.int32, (total, width), 0)
-        - reach
+        - 128
         - lax.broadcasted_iota(jnp.int32, (total, width), 1)
     ).astype(f32)
     table = jnp.where(lag <= jnp.minimum(columns, row), values, 0.0).astype(bf16)
-    first, last = table[:reach], table[reach + width :]
-    mid_ref[...] = table[reach : reach + width]
+    first, last = table[128 - reach : 128], table[128 + width : 128 + width + reach]
+    mid_ref[...] = table[128 : 128 + width]
     halo_ref[0] = jnp.concatenate([first, last])
     halo_ref[1] = jnp.concatenate([last, first])
 
 
 def exchange_kernel(
-    site_total, time_total, field, mid, halo, places, scale, pool, geo,
+    site_total, time_total, field_in, mid, halo, positions, scale, pool, geo, field, load,
     to_right, to_left, from_left, from_right, scales, edges,
     zsend, zrecv, gsend, grecv, psend, precv,
 ):
@@ -51,6 +70,8 @@
     reach = width // 4
     owned = 2 * blocks
 
+    fetch = pltpu.make_async_copy(field_in, field, load)
+    fetch.start()
     barrier = pltpu.get_barrier_semaphore()
     for o in range(1, site_total):
         pl.semaphore_signal(
@@ -74,11 +95,19 @@
         to_right[here, :] = jnp.where(lane, pltpu.roll(right_a, 64, 1), right_b).astype(bf16)
         to_left[here, :] = jnp.where(lane, left_b, pltpu.roll(left_a, 64, 1)).astype(bf16)
 
+    for j in range(2):
+        line = positions[pl.ds(j, 1), :].astype(f32) * (1.0 / 3.0)
+        for b in range(blocks):
+            geo[pl.ds(j * blocks + b, 1), :] = line[:, b * size : (b + 1) * size]
+    turned = jnp.transpose(scale[...])
+    for b in range(blocks):
+        scales[pl.ds(b * size, size), :] = jnp.broadcast_to(turned[:, b : b + 1], (size, 128))
+    fetch.wait()
     pack(0)
     for k in range(2):
         start = k * (blocks - CAP)
         for j in range(2):
-            edges[k, pl.ds(j * CAP, CAP), :] = places[pl.ds(j * blocks + start, CAP), :]
+            edges[k, pl.ds(j * CAP, CAP), :] = geo[pl.ds(j * blocks + start, CAP), :]
         edges[k, pl.ds(2 * CAP, 8 - 2 * CAP), :] = jnp.zeros((8 - 2 * CAP, 128), f32)
 
     pl.semaphore_wait(barrier, site_total + 1)
@@ -136,8 +165,6 @@
         lax.fori_loop(pieces[n][0], pieces[n][1], lambda c, _: (pack(c), 0)[1], 0)
         send(n)
 
-    geo[pl.ds(0, owned), :] = places[...]
-
     @pl.when(step == 0)
     def _():
         from_left[...] = jnp.zeros_like(from_left)
@@ -145,10 +172,6 @@
     @pl.when(step == time_total - 1)
     def _():
         from_right[...] = jnp.zeros_like(from_right)
-
-    turned = jnp.transpose(scale[...])
-    for b in range(blocks):
-        scales[pl.ds(b * size, size), :] = jnp.broadcast_to(turned[:, b : b + 1], (size, 128))
 
     def smooth(c):
         here = pl.ds(pl.multiple_of(c * group, group), group)
@@ -213,7 +236,7 @@
     site = lax.axis_index("site")
     blocks = scale.shape[0]
     size = tiles.shape[0]
-    slots = names.shape[0] // blocks
+    lanes = tiles.shape[1] // size
     width = out.shape[1]
     for ref, source in (
         (across, geo[pl.ds(0, blocks), :]),
@@ -225,7 +248,7 @@
             ref[pl.ds(b * size, size), :] = jnp.broadcast_to(turned[:, b : b + 1], (size, 128))
 
     def named(b, k):
-        name = names[b * slots + k]
+        name = names[b, k]
         owner = name // blocks
         within = name - owner * blocks
         window = jnp.where(owner > site, within, within - (blocks - CAP))
@@ -235,15 +258,16 @@
         second = jnp.where(near, blocks + within, 2 * blocks + 8 * owner + window + CAP)
         return place, first, second
 
-    def pair(b, k):
-        count = counts[b]
-        other = 2 * k + 1
-        live = other < count
-        return named(b, 2 * k), named(b, jnp.where(live, other, 2 * k)), live
+    def several(b, k):
+        last = counts[b] - 1
+        found = []
+        for j in range(lanes):
+            n = lanes * k + j
+            found.append((named(b, jnp.minimum(n, last)), jnp.where(n <= last, 1.0, 0.0)))
+        return found
 
     def build(b, k):
-        one, two, live = pair(b, k)
-        for j, (slot, weight) in enumerate(((one, 1.0), (two, jnp.where(live, 1.0, 0.0)))):
+        for j, (slot, weight) in enumerate(several(b, k)):
             x = geo[pl.ds(slot[1], 1), :]
             y = geo[pl.ds(slot[2], 1), :]
             for r in range(0, size, 32):
@@ -259,9 +283,8 @@
                 tiles[pl.ds(r, 32), pl.ds(j * size, size)] = value.astype(bf16)
 
     def multiply(b, k):
-        one, two, _ = pair(b, k)
         values = jnp.concatenate(
-            [pool[pl.ds(pl.multiple_of(s[0] * size, size), size), :] for s in (one, two)]
+            [pool[pl.ds(pl.multiple_of(s[0] * size, size), size), :] for s, _ in several(b, k)]
         )
         product = jnp.dot(tiles[...], values, preferred_element_type=f32)
         total = jnp.where(k > 0, acc[...], 0.0) + product
@@ -273,8 +296,8 @@
         weight = jnp.concatenate([scales[span, :]] * (width // 128), 1)
         out[span, :] = (total * weight).astype(bf16)
 
-    def pairs(b):
-        return (counts[b] + 1) // 2
+    def turns(b):
+        return (counts[b] + lanes - 1) // lanes
 
     build(0, 0)
 
@@ -284,7 +307,7 @@
             build(b, k)
             return 0
 
-        last = pairs(b)
+        last = turns(b)
         lax.fori_loop(1, last, inner, 0)
         finish(b, multiply(b, last - 1))
         build(jnp.minimum(b + 1, blocks - 1), 0)
@@ -298,27 +321,11 @@
     site_field, positions, site_scale, neighbor_blocks, neighbor_count, lag_values, time_band,
 ):
     rows, width = site_field.shape
-    blocks, slots = neighbor_blocks.shape
+    blocks = neighbor_count.shape[0]
     size = rows // blocks
     reach = lag_values.shape[0] - 1
     group = CAP * size
-    places = (positions.astype(f32) * (1.0 / 3.0)).reshape(2 * blocks, size)
     scale = site_scale.astype(f32).reshape(blocks, size)
-    series = jnp.concatenate(
-        [
-            lag_values[reach:],
-            jnp.zeros((2 * width - 2 * reach - 1,), f32),
-            lag_values[:0:-1],
-            lag_values[:reach],
-        ]
-    ).reshape(1, 2 * width)
-    start = lax.axis_index("tm") * width
-    padded = jnp.pad(time_band.astype(f32), (reach, reach))
-    around = lax.dynamic_slice_in_dim(padded, start, width + 2 * reach)
-    total = width + 2 * reach
-    band = jnp.concatenate(
-        [around, around[reach : reach + width], jnp.zeros((8 * 128 - total - width,), f32)]
-    ).reshape(8, 128)
     vmem = pl.BlockSpec(memory_space=pltpu.VMEM)
     smem = pl.BlockSpec(memory_space=pltpu.SMEM)
     mid, halo = pl.pallas_call(
@@ -329,17 +336,21 @@
         ],
         in_specs=[vmem] * 2,
         out_specs=[vmem] * 2,
+        scratch_shapes=[pltpu.VMEM((8, 128), f32)],
+        compiler_params=pltpu.CompilerParams(vmem_limit_bytes=12 * 2**20),
         name="table",
-    )(series, band)
+    )(lag_values.reshape(1, -1), time_band.reshape(-1, 128))
     pool, geo = pl.pallas_call(
         functools.partial(exchange_kernel, site_total, time_total),
         out_shape=[
             jax.ShapeDtypeStruct((rows + site_total * group, width), bf16),
             jax.ShapeDtypeStruct((2 * blocks + 8 * site_total, size), f32),
         ],
-        in_specs=[vmem] * 5,
+        in_specs=[pl.BlockSpec(memory_space=pltpu.HBM)] + [vmem] * 4,
         out_specs=[vmem] * 2,
         scratch_shapes=[
+            pltpu.VMEM((rows, width), bf16),
+            pltpu.SemaphoreType.DMA,
             pltpu.VMEM((rows // 2, 128), bf16),
             pltpu.VMEM((rows // 2, 128), bf16),
             pltpu.VMEM((rows // 2, 128), bf16),
@@ -357,7 +368,7 @@
             collective_id=0, has_side_effects=True, vmem_limit_bytes=24 * 2**20
         ),
         name="exchange",
-    )(site_field, mid, halo, places, scale)
+    )(site_field, mid, halo, positions, scale)
     return pl.pallas_call(
         combine_kernel,
         out_shape=jax.ShapeDtypeStruct((rows, width), bf16),
@@ -365,14 +376,14 @@
         out_specs=vmem,
         scratch_shapes=[
             pltpu.VMEM((size, width), f32),
-            pltpu.VMEM((size, 2 * size), bf16),
+            pltpu.VMEM((size, 4 * size), bf16),
             pltpu.VMEM((rows, 128), f32),
             pltpu.VMEM((rows, 128), f32),
             pltpu.VMEM((rows, 128), f32),
         ],
         compiler_params=pltpu.CompilerParams(vmem_limit_bytes=28 * 2**20),
         name="combine",
-    )(neighbor_blocks.reshape(-1), neighbor_count, pool, geo, scale)
+    )(neighbor_blocks, neighbor_count, pool, geo, scale)
 
 
 def solution(mesh):

time: 61.2 us -> 53.2 us (0.87)
  the two profiles are of different devices: /device:TPU:0 before, /device:TPU:1 now
where the time goes in v2:
time: 53.2 us; the launch traced here: 54 us
  Pallas kernels  48.8 us (92%)
  local copies, waits for them, and re-layouts  4.42 us (8%)
  other arithmetic  0.71 us (1%)
    pallas_call x1, Pallas kernels, shards(): pl.pallas_call(combine_kernel, out_shape=jax.ShapeDtypeStruct((rows, widt...  28.1 us
    pallas_call x1, Pallas kernels, shards(): pl.pallas_call(functools.partial(exchange_kernel, site_total, time_total)...  20.3 us
    unnamed x11, local copies, waits for them, and re-layouts  4.42 us

profile of v2, /device:TPU:1, one launch (start us, length us, event | category | flops | bytes accessed | tf_op | source)
XLA Modules:
  0.0 54.0 jit_solution(2320804592274515797)
XLA Ops:
  0.0 0.0 copy-start.3
  0.0 0.7 %bitcast_convert_fusion.scale = f32[32,128]{1,0:T(8,128)S(1)} fusion(bf16[4096]{0:T(1024)(128)(2,1)} %param.9), kind=kLoop, calls=%fused_computation | loop fusion | flops 4096 | bytes 24576 | tf_op jit(solution)/shard_map/reshape | solution.py:328
  0.7 0.8 %copy.8.names = s32[32,16]{1,0:T(8,128)S(1)} copy(s32[32,16]{0,1:T(8,128)} %param.10) | data formatting | bytes 4096 | tf_op args[3]
  1.5 0.0 copy-start.2
  1.5 0.7 %copy-done.2 = s32[1024]{0:T(1024)S(1)} copy-done((s32[1024]{0:T(1024)S(1)}, s32[1024]{0:T(1024)}, u32[]{:S(2)}) %copy-start.2) | copy-done | bytes 4120
  2.2 0.0 copy-start.4
  2.2 0.7 %copy-done.4 = f32[65]{0:T(128)S(1)} copy-done((f32[65]{0:T(128)S(1)}, f32[65]{0:T(128)}, u32[]{:S(2)}) %copy-start.4) | copy-done | bytes 284
  2.8 0.4 table.1
  3.2 0.0 copy-start
  3.2 1.6 %copy-done = bf16[4096,256]{1,0:T(8,128)(2,1)S(1)} copy-done((bf16[4096,256]{1,0:T(8,128)(2,1)S(1)}, bf16[4096,256]{1,0:T(8,128)(2,1)}, u32[]{:S(2)}) %copy-start) | copy-done | bytes 2097176
  4.8 0.0 copy-start.1
  4.8 0.7 %copy-done.1 = bf16[2,4096]{1,0:T(2,128)(2,1)S(1)} copy-done((bf16[2,4096]{1,0:T(2,128)(2,1)S(1)}, bf16[2,4096]{1,0:T(2,128)(2,1)}, u32[]{:S(2)}) %copy-start.1) | copy-done | bytes 16408
  5.5 20.3 %exchange.1 = (bf16[6144,256]{1,0:T(8,128)(2,1)S(1)}, f32[128,128]{1,0:T(8,128)S(1)}) custom-call(bf16[4096,256]{1,0:T(8,128)(2,1)S(1)} %copy-done, bf16[256,256]{1,0:T(8,128)(2,1)S(1)} %get-tuple-element.9.mid, bf16[2,128,256]{2,1,0:T(8,128)(2,1)S(1)} %get-tuple-element.10.halo, bf16[2,4096]{1,0:T(2,128)(2,1)S(1)} %copy-done.1, ...), custom_call_target="tpu_custom_call" | custom-call | tf_op jit(solution)/shard_map/exchange/pallas_call | solution.py:343
  25.9 0.0 copy-done.3
  25.9 28.1 %combine.1 = bf16[4096,256]{1,0:T(8,128)(2,1)} custom-call(s32[32,16]{1,0:T(8,128)S(1)} %copy.8.names, s32[32]{0:T(128)S(1)} %copy-done.3, bf16[6144,256]{1,0:T(8,128)(2,1)S(1)} %get-tuple-element.11.pool, f32[128,128]{1,0:T(8,128)S(1)} %get-tuple-element.12.geo, f32[32,128]{1,0:T(8,128)S(1)} %bitcast_convert_fusion.scale), custom_call_target="tpu_custom_call" | custom-call | tf_op jit(solution)/shard_map/combine/pallas_call | solution.py:372
Async XLA Ops:
  0.0 25.9 %copy-start.3 = (s32[32]{0:T(128)S(1)}, s32[32]{0:T(128)}, u32[]{:S(2)}) copy-start(s32[32]{0:T(128)} %counts.1) | copy-start | bytes 388
  1.5 0.7 %copy-start.2 = (s32[1024]{0:T(1024)S(1)}, s32[1024]{0:T(1024)}, u32[]{:S(2)}) copy-start(s32[1024]{0:T(1024)} %param.13) | copy-start | bytes 12292
  2.2 0.7 %copy-start.4 = (f32[65]{0:T(128)S(1)}, f32[65]{0:T(128)}, u32[]{:S(2)}) copy-start(f32[65]{0:T(128)} %param.12) | copy-start | bytes 784
  3.2 1.6 %copy-start = (bf16[4096,256]{1,0:T(8,128)(2,1)S(1)}, bf16[4096,256]{1,0:T(8,128)(2,1)}, u32[]{:S(2)}) copy-start(bf16[4096,256]{1,0:T(8,128)(2,1)} %field_in.1) | copy-start | bytes 6291460
  4.8 0.7 %copy-start.1 = (bf16[2,4096]{1,0:T(2,128)(2,1)S(1)}, bf16[2,4096]{1,0:T(2,128)(2,1)}, u32[]{:S(2)}) copy-start(bf16[2,4096]{1,0:T(2,128)(2,1)} %positions.1) | copy-start | bytes 49156

commit v3 on v2

--- a/solution.py
+++ b/solution.py
@@ -9,6 +9,7 @@
 from jax.sharding import PartitionSpec as P
 
 CAP = 2
+LANES = 4
 MESH = pl.DeviceIdType.MESH
 f32 = jnp.float32
 bf16 = jnp.bfloat16
@@ -56,8 +57,45 @@
     halo_ref[1] = jnp.concatenate([last, first])
 
 
+def several(names, counts, site, b, k, blocks):
+    last = jnp.maximum(counts[b] - 1, 0)
+    found = []
+    for j in range(LANES):
+        n = LANES * k + j
+        name = names[b, jnp.minimum(n, last)]
+        owner = name // blocks
+        within = name - owner * blocks
+        window = jnp.where(owner > site, within, within - (blocks - CAP))
+        window = jnp.clip(window, 0, CAP - 1)
+        near = owner == site
+        place = jnp.where(near, within, blocks + owner * CAP + window)
+        first = jnp.where(near, within, 2 * blocks + 8 * owner + window)
+        second = jnp.where(near, blocks + within, 2 * blocks + 8 * owner + window + CAP)
+        found.append((place, first, second, jnp.where(n <= last, 1.0, 0.0)))
+    return found
+
+
+def build_tiles(found, b, geo, across, upward, tiles):
+    size = tiles.shape[0]
+    for j, (_, first, second, weight) in enumerate(found):
+        x = geo[pl.ds(first, 1), :]
+        y = geo[pl.ds(second, 1), :]
+        for r in range(0, size, 32):
+            span = pl.ds(pl.multiple_of(b * size + r, 32), 32)
+            dx = across[span, :] - x
+            dy = upward[span, :] - y
+            square = dx * dx + dy * dy
+            d = square * lax.rsqrt(jnp.maximum(square, 1e-30))
+            t = jnp.maximum(1.0 - d, 0.0)
+            t = t * t
+            value = jnp.exp2(d * (-15.0 * math.log2(math.e))) * (t * t)
+            value = value * (d * (4.0 * weight) + weight)
+            tiles[pl.ds(r, 32), pl.ds(j * size, size)] = value.astype(bf16)
+
+
 def exchange_kernel(
-    site_total, time_total, field_in, mid, halo, positions, scale, pool, geo, field, load,
+    site_total, time_total, field_in, mid, halo, positions, scale, names, counts,
+    pool, geo, ready, across_rows, upward_rows, field, load,
     to_right, to_left, from_left, from_right, scales, edges,
     zsend, zrecv, gsend, grecv, psend, precv,
 ):
@@ -109,6 +147,7 @@
         for j in range(2):
             edges[k, pl.ds(j * CAP, CAP), :] = geo[pl.ds(j * blocks + start, CAP), :]
         edges[k, pl.ds(2 * CAP, 8 - 2 * CAP), :] = jnp.zeros((8 - 2 * CAP, 128), f32)
+    geo[pl.ds(pl.multiple_of(owned + 8 * site, 8), 8), :] = jnp.zeros((8, 128), f32)
 
     pl.semaphore_wait(barrier, site_total + 1)
 
@@ -173,6 +212,11 @@
     def _():
         from_right[...] = jnp.zeros_like(from_right)
 
+    for ref, base in ((across_rows, 0), (upward_rows, blocks)):
+        turned = jnp.transpose(geo[pl.ds(base, blocks), :])
+        for b in range(blocks):
+            ref[pl.ds(b * size, size), :] = jnp.broadcast_to(turned[:, b : b + 1], (size, 128))
+
     def smooth(c):
         here = pl.ds(pl.multiple_of(c * group, group), group)
         there = pl.ds(pl.multiple_of(rows - (c + 1) * group, group), group)
@@ -200,6 +244,29 @@
     smooth(0)
     for o in range(1, site_total):
         across(o).start()
+
+    def landed(o, into, base, length, sem):
+        origin = lax.rem(site + site_total - o, site_total)
+        landing = into.at[pl.ds(pl.multiple_of(base + origin * length, 8), length)]
+        pltpu.make_async_remote_copy(
+            src_ref=landing,
+            dst_ref=landing,
+            send_sem=sem.at[o - 1],
+            recv_sem=sem.at[o - 1],
+            device_id={"site": origin},
+            device_id_type=MESH,
+        ).wait_recv()
+
+    for o in range(1, site_total):
+        points(o).wait_send()
+        landed(o, geo, owned, 8, precv)
+
+    def prepare(b, _):
+        found = several(names, counts, site, b, 0, blocks)
+        build_tiles(found, b, geo, across_rows, upward_rows, ready.at[b])
+        return 0
+
+    lax.fori_loop(0, blocks, prepare, 0)
     for n in range(1, len(pieces)):
         receive(n)
         lax.fori_loop(pieces[n][0], pieces[n][1], lambda c, _: (smooth(c), 0)[1], 0)
@@ -215,28 +282,14 @@
             sideways(n, False).wait_send()
 
     for o in range(1, site_total):
-        for copy, into, base, length, sem in (
-            (points(o), geo, owned, 8, precv),
-            (across(o), pool, rows, group, grecv),
-        ):
-            copy.wait_send()
-            origin = lax.rem(site + site_total - o, site_total)
-            landing = into.at[pl.ds(pl.multiple_of(base + origin * length, 8), length)]
-            pltpu.make_async_remote_copy(
-                src_ref=landing,
-                dst_ref=landing,
-                send_sem=sem.at[o - 1],
-                recv_sem=sem.at[o - 1],
-                device_id={"site": origin},
-                device_id_type=MESH,
-            ).wait_recv()
-
-
-def combine_kernel(names, counts, pool, geo, scale, out, acc, tiles, across, upward, scales):
+        across(o).wait_send()
+        landed(o, pool, rows, group, grecv)
+
+
+def combine_kernel(names, counts, pool, geo, ready, scale, out, acc, tiles, across, upward, scales):
     site = lax.axis_index("site")
     blocks = scale.shape[0]
     size = tiles.shape[0]
-    lanes = tiles.shape[1] // size
     width = out.shape[1]
     for ref, source in (
         (across, geo[pl.ds(0, blocks), :]),
@@ -247,59 +300,32 @@
         for b in range(blocks):
             ref[pl.ds(b * size, size), :] = jnp.broadcast_to(turned[:, b : b + 1], (size, 128))
 
-    def named(b, k):
-        name = names[b, k]
-        owner = name // blocks
-        within = name - owner * blocks
-        window = jnp.where(owner > site, within, within - (blocks - CAP))
-        near = owner == site
-        place = jnp.where(near, within, blocks + owner * CAP + window)
-        first = jnp.where(near, within, 2 * blocks + 8 * owner + window)
-        second = jnp.where(near, blocks + within, 2 * blocks + 8 * owner + window + CAP)
-        return place, first, second
-
-    def several(b, k):
-        last = counts[b] - 1
-        found = []
-        for j in range(lanes):
-            n = lanes * k + j
-            found.append((named(b, jnp.minimum(n, last)), jnp.where(n <= last, 1.0, 0.0)))
-        return found
-
     def build(b, k):
-        for j, (slot, weight) in enumerate(several(b, k)):
-            x = geo[pl.ds(slot[1], 1), :]
-            y = geo[pl.ds(slot[2], 1), :]
-            for r in range(0, size, 32):
-                span = pl.ds(pl.multiple_of(b * size + r, 32), 32)
-                dx = across[span, :] - x
-                dy = upward[span, :] - y
-                square = dx * dx + dy * dy
-                d = square * lax.rsqrt(jnp.maximum(square, 1e-30))
-                t = jnp.maximum(1.0 - d, 0.0)
-                t = t * t
-                value = jnp.exp2(d * (-15.0 * math.log2(math.e))) * (t * t)
-                value = value * (d * (4.0 * weight) + weight)
-                tiles[pl.ds(r, 32), pl.ds(j * size, size)] = value.astype(bf16)
+        found = several(names, counts, site, b, k, blocks)
+        build_tiles(found, b, geo, across, upward, tiles)
+
+    def values(b, k):
+        found = several(names, counts, site, b, k, blocks)
+        return jnp.concatenate(
+            [pool[pl.ds(pl.multiple_of(s[0] * size, size), size), :] for s in found]
+        )
 
     def multiply(b, k):
-        values = jnp.concatenate(
-            [pool[pl.ds(pl.multiple_of(s[0] * size, size), size), :] for s, _ in several(b, k)]
-        )
-        product = jnp.dot(tiles[...], values, preferred_element_type=f32)
-        total = jnp.where(k > 0, acc[...], 0.0) + product
+        product = jnp.dot(tiles[...], values(b, k), preferred_element_type=f32)
+        total = jnp.where(k > 1, acc[...], 0.0) + product
         acc[...] = total
         return total
 
     def finish(b, total):
+        total = total + jnp.dot(ready[b], values(b, 0), preferred_element_type=f32)
         span = pl.ds(pl.multiple_of(b * size, size), size)
         weight = jnp.concatenate([scales[span, :]] * (width // 128), 1)
         out[span, :] = (total * weight).astype(bf16)
 
     def turns(b):
-        return (counts[b] + lanes - 1) // lanes
-
-    build(0, 0)
+        return jnp.maximum((counts[b] + LANES - 1) // LANES, 2)
+
+    build(0, 1)
 
     def block(b, _):
         def inner(k, _):
@@ -308,9 +334,9 @@
             return 0
 
         last = turns(b)
-        lax.fori_loop(1, last, inner, 0)
+        lax.fori_loop(2, last, inner, 0)
         finish(b, multiply(b, last - 1))
-        build(jnp.minimum(b + 1, blocks - 1), 0)
+        build(jnp.minimum(b + 1, blocks - 1), 1)
         return 0
 
     lax.fori_loop(0, blocks, block, 0)
@@ -340,15 +366,18 @@
         compiler_params=pltpu.CompilerParams(vmem_limit_bytes=12 * 2**20),
         name="table",
     )(lag_values.reshape(1, -1), time_band.reshape(-1, 128))
-    pool, geo = pl.pallas_call(
+    pool, geo, ready = pl.pallas_call(
         functools.partial(exchange_kernel, site_total, time_total),
         out_shape=[
             jax.ShapeDtypeStruct((rows + site_total * group, width), bf16),
             jax.ShapeDtypeStruct((2 * blocks + 8 * site_total, size), f32),
+            jax.ShapeDtypeStruct((blocks, size, LANES * size), bf16),
         ],
-        in_specs=[pl.BlockSpec(memory_space=pltpu.HBM)] + [vmem] * 4,
-        out_specs=[vmem] * 2,
+        in_specs=[pl.BlockSpec(memory_space=pltpu.HBM)] + [vmem] * 4 + [smem] * 2,
+        out_specs=[vmem] * 3,
         scratch_shapes=[
+            pltpu.VMEM((rows, 128), f32),
+            pltpu.VMEM((rows, 128), f32),
             pltpu.VMEM((rows, width), bf16),
             pltpu.SemaphoreType.DMA,
             pltpu.VMEM((rows // 2, 128), bf16),
@@ -368,22 +397,22 @@
             collective_id=0, has_side_effects=True, vmem_limit_bytes=24 * 2**20
         ),
         name="exchange",
-    )(site_field, mid, halo, positions, scale)
+    )(site_field, mid, halo, positions, scale, neighbor_blocks, neighbor_count)
     return pl.pallas_call(
         combine_kernel,
         out_shape=jax.ShapeDtypeStruct((rows, width), bf16),
-        in_specs=[smem] * 2 + [vmem] * 3,
+        in_specs=[smem] * 2 + [vmem] * 4,
         out_specs=vmem,
         scratch_shapes=[
             pltpu.VMEM((size, width), f32),
-            pltpu.VMEM((size, 4 * size), bf16),
+            pltpu.VMEM((size, LANES * size), bf16),
             pltpu.VMEM((rows, 128), f32),
             pltpu.VMEM((rows, 128), f32),
             pltpu.VMEM((rows, 128), f32),
         ],
         compiler_params=pltpu.CompilerParams(vmem_limit_bytes=28 * 2**20),
         name="combine",
-    )(neighbor_blocks, neighbor_count, pool, geo, scale)
+    )(neighbor_blocks, neighbor_count, pool, geo, ready, scale)
 
 
 def solution(mesh):

time: 53.2 us -> 51.4 us (0.966); the launches traced: 54 us -> 50.7 us
  Pallas kernels: 48.8 us -> 44.3 us
  local copies, waits for them, and re-layouts: 4.42 us -> 5.72 us
    pallas_call x1, Pallas kernels: 28.1 us -> 22.4 us  [shards(): pl.pallas_call(combine_kernel, out_shape=jax.ShapeDtypeStruct((rows, widt...]
    unnamed x11 -> x13, local copies, waits for them, and re-layouts: 4.42 us -> 5.72 us
    pallas_call x1, Pallas kernels: 20.3 us -> 21.4 us  [shards(): pl.pallas_call(functools.partial(exchange_kernel, site_total, time_total)...]
where the time goes in v3:
time: 51.4 us; the launch traced here: 50.7 us
  Pallas kernels  44.3 us (86%)
  local copies, waits for them, and re-layouts  5.72 us (11%)
  other arithmetic  0.7 us (1%)
    pallas_call x1, Pallas kernels, shards(): pl.pallas_call(combine_kernel, out_shape=jax.ShapeDtypeStruct((rows, widt...  22.4 us
    pallas_call x1, Pallas kernels, shards(): pl.pallas_call(functools.partial(exchange_kernel, site_total, time_total)...  21.4 us
    unnamed x13, local copies, waits for them, and re-layouts  5.72 us

profile of v3, /device:TPU:1, one launch (start us, length us, event | category | flops | bytes accessed | tf_op | source)
XLA Modules:
  0.0 50.7 jit_solution(17983681530496063496)
XLA Ops:
  0.0 0.7 %bitcast_convert_fusion.scale = f32[32,128]{1,0:T(8,128)S(1)} fusion(bf16[4096]{0:T(1024)(128)(2,1)} %param.9), kind=kLoop, calls=%fused_computation | loop fusion | flops 4096 | bytes 24576 | tf_op jit(solution)/shard_map/reshape | solution.py:354
  0.7 0.8 %copy.9.names = s32[32,16]{1,0:T(8,128)S(1)} copy(s32[32,16]{0,1:T(8,128)} %param.10) | data formatting | bytes 4096 | tf_op args[3]
  1.5 0.0 copy-start.2
  1.5 0.7 %copy-done.2 = s32[1024]{0:T(1024)S(1)} copy-done((s32[1024]{0:T(1024)S(1)}, s32[1024]{0:T(1024)}, u32[]{:S(2)}) %copy-start.2) | copy-done | bytes 4120
  2.2 0.0 copy-start.5
  2.2 0.7 %copy-done.5 = f32[65]{0:T(128)S(1)} copy-done((f32[65]{0:T(128)S(1)}, f32[65]{0:T(128)}, u32[]{:S(2)}) %copy-start.5) | copy-done | bytes 284
  2.8 0.4 table.1
  3.2 0.0 copy-start
  3.2 1.6 %copy-done = bf16[4096,256]{1,0:T(8,128)(2,1)S(1)} copy-done((bf16[4096,256]{1,0:T(8,128)(2,1)S(1)}, bf16[4096,256]{1,0:T(8,128)(2,1)}, u32[]{:S(2)}) %copy-start) | copy-done | bytes 2097176
  4.8 0.0 copy-start.1
  4.8 0.7 %copy-done.1 = bf16[2,4096]{1,0:T(2,128)(2,1)S(1)} copy-done((bf16[2,4096]{1,0:T(2,128)(2,1)S(1)}, bf16[2,4096]{1,0:T(2,128)(2,1)}, u32[]{:S(2)}) %copy-start.1) | copy-done | bytes 16408
  5.5 0.0 copy-start.3
  5.5 0.7 %copy-done.3 = s32[32]{0:T(128)S(1)} copy-done((s32[32]{0:T(128)S(1)}, s32[32]{0:T(128)}, u32[]{:S(2)}) %copy-start.3) | copy-done | bytes 152
  6.2 21.4 %exchange.1 = (bf16[6144,256]{1,0:T(8,128)(2,1)S(1)}, f32[128,128]{1,0:T(8,128)S(1)}, bf16[32,128,512]{2,1,0:T(8,128)(2,1)S(1)}) custom-call(bf16[4096,256]{1,0:T(8,128)(2,1)S(1)} %copy-done, bf16[256,256]{1,0:T(8,128)(2,1)S(1)} %get-tuple-element.10.mid, bf16[2,128,256]{2,1,0:T(8,128)(2,1)S(1)} %get-tuple-element.11.halo, bf16[2,4096]{1,0:T(2,128)(2,1)S(1)} %copy-done.1, ...), custom_call_target="tpu_custom_call" | custom-call | tf_op jit(solution)/shard_map/exchange/pallas_call | solution.py:369
  27.6 0.0 copy-start.4
  27.6 0.6 %copy-done.4 = s32[32]{0:T(128)S(1)} copy-done((s32[32]{0:T(128)S(1)}, s32[32]{0:T(128)}, u32[]{:S(2)}) %copy-start.4) | copy-done | bytes 152
  28.3 22.4 %combine.1 = bf16[4096,256]{1,0:T(8,128)(2,1)} custom-call(s32[32,16]{1,0:T(8,128)S(1)} %copy.9.names, s32[32]{0:T(128)S(1)} %copy-done.4, bf16[6144,256]{1,0:T(8,128)(2,1)S(1)} %get-tuple-element.12.pool, f32[128,128]{1,0:T(8,128)S(1)} %get-tuple-element.13.geo, bf16[32,128,512]{2,1,0:T(8,128)(2,1)S(1)} %get-tuple-element.14.ready, ...), custom_call_target="tpu_custom_call" | custom-call | tf_op jit(solution)/shard_map/combine/pallas_call | solution.py:401
Async XLA Ops:
  1.5 0.7 %copy-start.2 = (s32[1024]{0:T(1024)S(1)}, s32[1024]{0:T(1024)}, u32[]{:S(2)}) copy-start(s32[1024]{0:T(1024)} %param.13) | copy-start | bytes 12292
  2.2 0.7 %copy-start.5 = (f32[65]{0:T(128)S(1)}, f32[65]{0:T(128)}, u32[]{:S(2)}) copy-start(f32[65]{0:T(128)} %param.12) | copy-start | bytes 784
  3.2 1.6 %copy-start = (bf16[4096,256]{1,0:T(8,128)(2,1)S(1)}, bf16[4096,256]{1,0:T(8,128)(2,1)}, u32[]{:S(2)}) copy-start(bf16[4096,256]{1,0:T(8,128)(2,1)} %field_in.1) | copy-start | bytes 6291460
  4.8 0.7 %copy-start.1 = (bf16[2,4096]{1,0:T(2,128)(2,1)S(1)}, bf16[2,4096]{1,0:T(2,128)(2,1)}, u32[]{:S(2)}) copy-start(bf16[2,4096]{1,0:T(2,128)(2,1)} %positions.1) | copy-start | bytes 49156
  5.5 0.7 %copy-start.3 = (s32[32]{0:T(128)S(1)}, s32[32]{0:T(128)}, u32[]{:S(2)}) copy-start(s32[32]{0:T(128)} %counts.3) | copy-start | bytes 388
  27.6 0.7 %copy-start.4 = (s32[32]{0:T(128)S(1)}, s32[32]{0:T(128)}, u32[]{:S(2)}) copy-start(s32[32]{0:T(128)} %counts.3) | copy-start | bytes 388

commit v4 on v2

--- a/solution.py
+++ b/solution.py
@@ -376,7 +376,7 @@
         out_specs=vmem,
         scratch_shapes=[
             pltpu.VMEM((size, width), f32),
-            pltpu.VMEM((size, 4 * size), bf16),
+            pltpu.VMEM((size, 6 * size), bf16),
             pltpu.VMEM((rows, 128), f32),
             pltpu.VMEM((rows, 128), f32),
             pltpu.VMEM((rows, 128), f32),

time: 53.2 us -> 55.8 us (1.049)
  the two profiles are of different devices: /device:TPU:1 before, /device:TPU:15 now
where the time goes in v4:
time: 55.8 us; the launch traced here: 54.8 us
  Pallas kernels  49.6 us (89%)
  local copies, waits for them, and re-layouts  4.42 us (8%)
  other arithmetic  0.71 us (1%)
    pallas_call x1, Pallas kernels, shards(): pl.pallas_call(combine_kernel, out_shape=jax.ShapeDtypeStruct((rows, widt...  29.8 us
    pallas_call x1, Pallas kernels, shards(): pl.pallas_call(functools.partial(exchange_kernel, site_total, time_total)...  19.4 us
    unnamed x11, local copies, waits for them, and re-layouts  4.42 us

profile of v4, /device:TPU:15, one launch (start us, length us, event | category | flops | bytes accessed | tf_op | source)
XLA Modules:
  0.0 54.8 jit_solution(3057132565125317484)
XLA Ops:
  0.0 0.0 copy-start.3
  0.0 0.7 %bitcast_convert_fusion.scale = f32[32,128]{1,0:T(8,128)S(1)} fusion(bf16[4096]{0:T(1024)(128)(2,1)} %param.9), kind=kLoop, calls=%fused_computation | loop fusion | flops 4096 | bytes 24576 | tf_op jit(solution)/shard_map/reshape | solution.py:328
  0.7 0.8 %copy.8.names = s32[32,16]{1,0:T(8,128)S(1)} copy(s32[32,16]{0,1:T(8,128)} %param.10) | data formatting | bytes 4096 | tf_op args[3]
  1.5 0.0 copy-start.2
  1.5 0.7 %copy-done.2 = s32[1024]{0:T(1024)S(1)} copy-done((s32[1024]{0:T(1024)S(1)}, s32[1024]{0:T(1024)}, u32[]{:S(2)}) %copy-start.2) | copy-done | bytes 4120
  2.2 0.0 copy-start.4
  2.2 0.7 %copy-done.4 = f32[65]{0:T(128)S(1)} copy-done((f32[65]{0:T(128)S(1)}, f32[65]{0:T(128)}, u32[]{:S(2)}) %copy-start.4) | copy-done | bytes 284
  2.8 0.4 table.1
  3.2 0.0 copy-start
  3.2 1.6 %copy-done = bf16[4096,256]{1,0:T(8,128)(2,1)S(1)} copy-done((bf16[4096,256]{1,0:T(8,128)(2,1)S(1)}, bf16[4096,256]{1,0:T(8,128)(2,1)}, u32[]{:S(2)}) %copy-start) | copy-done | bytes 2097176
  4.8 0.0 copy-start.1
  4.8 0.7 %copy-done.1 = bf16[2,4096]{1,0:T(2,128)(2,1)S(1)} copy-done((bf16[2,4096]{1,0:T(2,128)(2,1)S(1)}, bf16[2,4096]{1,0:T(2,128)(2,1)}, u32[]{:S(2)}) %copy-start.1) | copy-done | bytes 16408
  5.5 19.4 %exchange.1 = (bf16[6144,256]{1,0:T(8,128)(2,1)S(1)}, f32[128,128]{1,0:T(8,128)S(1)}) custom-call(bf16[4096,256]{1,0:T(8,128)(2,1)S(1)} %copy-done, bf16[256,256]{1,0:T(8,128)(2,1)S(1)} %get-tuple-element.9.mid, bf16[2,128,256]{2,1,0:T(8,128)(2,1)S(1)} %get-tuple-element.10.halo, bf16[2,4096]{1,0:T(2,128)(2,1)S(1)} %copy-done.1, ...), custom_call_target="tpu_custom_call" | custom-call | tf_op jit(solution)/shard_map/exchange/pallas_call | solution.py:343
  25.0 0.0 copy-done.3
  25.0 29.8 %combine.1 = bf16[4096,256]{1,0:T(8,128)(2,1)} custom-call(s32[32,16]{1,0:T(8,128)S(1)} %copy.8.names, s32[32]{0:T(128)S(1)} %copy-done.3, bf16[6144,256]{1,0:T(8,128)(2,1)S(1)} %get-tuple-element.11.pool, f32[128,128]{1,0:T(8,128)S(1)} %get-tuple-element.12.geo, f32[32,128]{1,0:T(8,128)S(1)} %bitcast_convert_fusion.scale), custom_call_target="tpu_custom_call" | custom-call | tf_op jit(solution)/shard_map/combine/pallas_call | solution.py:372
Async XLA Ops:
  0.0 25.0 %copy-start.3 = (s32[32]{0:T(128)S(1)}, s32[32]{0:T(128)}, u32[]{:S(2)}) copy-start(s32[32]{0:T(128)} %counts.1) | copy-start | bytes 388
  1.5 0.7 %copy-start.2 = (s32[1024]{0:T(1024)S(1)}, s32[1024]{0:T(1024)}, u32[]{:S(2)}) copy-start(s32[1024]{0:T(1024)} %param.13) | copy-start | bytes 12292
  2.2 0.7 %copy-start.4 = (f32[65]{0:T(128)S(1)}, f32[65]{0:T(128)}, u32[]{:S(2)}) copy-start(f32[65]{0:T(128)} %param.12) | copy-start | bytes 784
  3.2 1.6 %copy-start = (bf16[4096,256]{1,0:T(8,128)(2,1)S(1)}, bf16[4096,256]{1,0:T(8,128)(2,1)}, u32[]{:S(2)}) copy-start(bf16[4096,256]{1,0:T(8,128)(2,1)} %field_in.1) | copy-start | bytes 6291460
  4.8 0.7 %copy-start.1 = (bf16[2,4096]{1,0:T(2,128)(2,1)S(1)}, bf16[2,4096]{1,0:T(2,128)(2,1)}, u32[]{:S(2)}) copy-start(bf16[2,4096]{1,0:T(2,128)(2,1)} %positions.1) | copy-start | bytes 49156
